TPU v7x, 32 devices: a whole 2x2x4 slice. The times are simulated.
32 devices in a mesh: gx: 8 (over z, x), gy: 4 (over y, core).
Axes of the slice: x: 2, y: 2, z: 4, core: 2. Of those that a mesh axis runs over, the one named last changes fastest.
Arguments:
- rhs: float32 [32, 32, 512], P('gx', 'gy'), may hold values from -6 to 6
- alpha: float32 [32, 32, 512], P('gx', 'gy'), may hold values from 0.0001 to 4
- beta_x: float32 [32, 32, 512], P('gx', 'gy'), may hold values from 0.5 to 2
- beta_y: float32 [32, 32, 512], P('gx', 'gy'), may hold values from 0.5 to 2
- beta_z: float32 [32, 32, 512], P('gx', 'gy'), may hold values from 0.5 to 2
Outputs:
- fine_solution: float32 [32, 32, 512], P('gx', 'gy')
- coarse_correction: float32 [8, 8, 128], P('gx', 'gy')
All inputs are finite; a program needn't handle non-finite values.
Results may differ from a plain program's by a relative error of at most 0.00002.
Values sent between devices are 32-bit elements; how exact they have to be, the bound alone decides.
A program may use at most 64 MiB of HBM per device.

v0:
```python
import jax
import jax.numpy as jnp
from jax import lax
from jax.sharding import PartitionSpec as P

SWEEPS = 4
COARSE_SWEEPS = 8


def extended(value, sides, width):
    for axis, dim in sides:
        count, length = (lax.axis_size(axis), value.shape[dim])
        up = [(i, (i + 1) % count) for i in range(count - 1)]
        down = [(j, i) for i, j in up]
        last = lax.slice_in_dim(value, length - width, length, axis=dim)
        leading = lax.slice_in_dim(value, 0, width, axis=dim)
        before = lax.ppermute(last, axis, up)
        after = lax.ppermute(leading, axis, down)
        value = jnp.concatenate([before, value, after], axis=dim)
    return value


def passed_along(value, axis, steps):
    count = lax.axis_size(axis)
    leading, last = (max(0, -steps), min(count, count - steps))
    return lax.ppermute(value, axis, [(source, source + steps) for source in range(leading, last)])


def upper_faces(beta, axis_pos):
    rest = lax.slice_in_dim(beta, 1, beta.shape[axis_pos], axis=axis_pos)
    zero_layer = jnp.zeros_like(lax.slice_in_dim(beta, 0, 1, axis=axis_pos))
    return jnp.concatenate([rest, zero_layer], axis=axis_pos)


def coarsen_face(faces, axis_pos, upper):
    size_x, size_y, size_z = faces.shape
    blocks = faces.reshape(size_x // 2, 2, size_y // 2, 2, size_z // 2, 2)
    taken = 2 * axis_pos + 1
    picked = jnp.take(blocks, upper, axis=taken)
    others = tuple((pair - 1 if pair > taken else pair for pair in (1, 3, 5) if pair != taken))
    return jnp.mean(picked, axis=others) * 0.25


def coarsen_all(faces):
    return tuple((coarsen_face(faces[number], number // 2, number % 2) for number in range(6)))


def restrict(field):
    size_x, size_y, size_z = field.shape
    return jnp.mean(field.reshape(size_x // 2, 2, size_y // 2, 2, size_z // 2, 2), axis=(1, 3, 5))


def prolong(field):
    return jnp.repeat(jnp.repeat(jnp.repeat(field, 2, 0), 2, 1), 2, 2)


def beside_sum(padded, faces):
    total = faces[0] * padded[:-2, 1:-1, 1:-1] + faces[1] * padded[2:, 1:-1, 1:-1]
    total = total + faces[2] * padded[1:-1, :-2, 1:-1] + faces[3] * padded[1:-1, 2:, 1:-1]
    total = total + faces[4] * padded[1:-1, 1:-1, :-2] + faces[5] * padded[1:-1, 1:-1, 2:]
    return total


def diagonal_of(cell_coef, faces):
    total = cell_coef
    for face in faces:
        total = total + face
    return total


def red_cells(shape, offset_x, offset_y):
    index_x = jnp.arange(shape[0], dtype=jnp.int32) + offset_x
    index_y = jnp.arange(shape[1], dtype=jnp.int32) + offset_y
    index_z = jnp.arange(shape[2], dtype=jnp.int32)
    return (index_x[:, None, None] + index_y[None, :, None] + index_z[None, None, :]) % 2 == 0


def extend_fine(field):
    padded = extended(field, (("gx", 0), ("gy", 1)), 1)
    return jnp.pad(padded, ((0, 0), (0, 0), (1, 1)))


def extend_residual(field):
    padded = extended(field, (("gx", 0), ("gy", 1)), 1)
    return jnp.pad(padded, ((0, 0), (0, 0), (1, 1)))


def extend_grid(field):
    padded = extended(field, (("gx", 0), ("gy", 1)), 1)
    return jnp.pad(padded, ((0, 0), (0, 0), (1, 1)))


def smooth(field, source, inverse, faces, red_mask, count, extend):

    def one_sweep(sweep_index, current):
        for colour in (True, False):
            beside = beside_sum(extend(current), faces)
            current = jnp.where(red_mask == colour, (source + beside) * inverse, current)
        return current

    return lax.fori_loop(0, count, one_sweep, field)


def residual_of(field, source, diagonal, faces):
    return source - (diagonal * field - beside_sum(extend_residual(field), faces))


def local_red(shape):
    return red_cells(shape, lax.axis_index("gx") * shape[0], lax.axis_index("gy") * shape[1])


def smooth_level(source, inverse, faces, count):
    return smooth(
        jnp.zeros_like(source), source, inverse, faces, local_red(source.shape), count, extend_fine
    )


def on_device(rhs, alpha, beta_x, beta_y, beta_z):
    next_x = passed_along(beta_x[0:1], "gx", -1)
    next_y = passed_along(beta_y[:, 0:1], "gy", -1)
    faces_fine = (
        beta_x,
        jnp.concatenate([beta_x[1:], next_x], 0),
        beta_y,
        jnp.concatenate([beta_y[:, 1:], next_y], 1),
        beta_z,
        upper_faces(beta_z, 2),
    )
    diagonal_fine = diagonal_of(alpha, faces_fine)
    smoothed = smooth_level(rhs, 1.0 / diagonal_fine, faces_fine, SWEEPS)
    source_mid = restrict(residual_of(smoothed, rhs, diagonal_fine, faces_fine))
    coef_mid = restrict(alpha)
    faces_mid = coarsen_all(faces_fine)
    diagonal_mid = diagonal_of(coef_mid, faces_mid)
    level_mid = smooth_level(source_mid, 1.0 / diagonal_mid, faces_mid, SWEEPS)
    source_low = restrict(residual_of(level_mid, source_mid, diagonal_mid, faces_mid))
    coef_low = restrict(coef_mid)
    faces_low = coarsen_all(faces_mid)
    inverse_low = 1.0 / diagonal_of(coef_low, faces_low)
    coarse = smooth(
        jnp.zeros_like(source_low),
        source_low,
        inverse_low,
        faces_low,
        local_red(source_low.shape),
        COARSE_SWEEPS,
        extend_grid,
    )
    corrected = level_mid + prolong(coarse)
    return (smoothed + prolong(corrected), coarse)


def solution(mesh):
    placed = (
        P("gx", "gy", None),
        P("gx", "gy", None),
        P("gx", "gy", None),
        P("gx", "gy", None),
        P("gx", "gy", None),
    )
    return jax.shard_map(
        on_device,
        mesh=mesh,
        in_specs=placed,
        out_specs=(P("gx", "gy", None), P("gx", "gy", None)),
        check_vma=False,
    )
```

profile of v0, /device:TPU:1, one launch (start us, length us, event | category | flops | bytes accessed | tf_op | source)
XLA Modules:
  0.0 606.5 jit_solution(8108328387701038732)
XLA Ops:
  5.5 6.3 %reshape.453 = f32[2,2,4,2,256,2]{5,4,3,2,1,0:T(8,128)} reshape(f32[4,8,512]{2,1,0:T(8,128)} %param.38) | data formatting | bytes 131072 | tf_op jit(solution)/shard_map/reshape | solution.py:37
  11.9 5.5 reshape.451
  17.4 5.5 reshape.455
  29.0 5.5 reshape.458
  37.2 5.5 reshape.454
  42.7 5.5 reshape.456
  48.2 125.6 %while.54 = (s32[]{:T(128)}, f32[4,8,512]{2,1,0:T(8,128)S(1)}, f32[4,8,512]{2,1,0:T(8,128)S(1)}, f32[4,8,512]{2,1,0:T(8,128)S(1)}, f32[4,8,512]{2,1,0:T(8,128)S(...) while((s32[]{:T(128)}, f32[4,8,512]{2,1,0:T(8,128)S(1)}, ...), condition=%wide.region_1.2_spmd.clone, body=%wide.region_0.1_spmd.clone.sunk | while | flops 1944387 | bytes 3147399 | solution.py:101
  49.6 5.8 collective-permute-start.1
  80.6 5.4 collective-permute-start.1
  96.3 5.4 collective-permute-start.5
  112.1 5.4 collective-permute-start.1
  127.9 5.4 collective-permute-start.5
  143.6 5.4 collective-permute-start.1
  159.4 5.4 collective-permute-start.5
  184.0 5.5 reshape.452
  206.1 5.5 reshape.457
  218.7 121.6 %while.55 = (s32[]{:T(128)}, f32[2,4,256]{2,1,0:T(4,128)S(1)}, f32[2,4,256]{2,1,0:T(4,128)S(1)}, f32[2,4,256]{2,1,0:T(4,128)S(1)}, f32[2,4,256]{2,1,0:T(4,128)S(...) while((s32[]{:T(128)}, f32[2,4,256]{2,1,0:T(4,128)S(1)}, ...), condition=%wide.region_11.18_spmd.clone, body=%wide.region_10.17_spmd.clone.sunk | while | flops 304259 | bytes 557959 | solution.py:101
  249.0 5.4 collective-permute-start.9
  264.4 5.4 collective-permute-start.13
  279.9 5.4 collective-permute-start.9
  295.3 5.4 collective-permute-start.13
  310.7 5.4 collective-permute-start.9
  326.1 5.4 collective-permute-start.13
  362.0 242.4 %while.56 = (s32[]{:T(128)}, f32[1,2,128]{2,1,0:T(2,128)S(1)}, f32[1,2,128]{2,1,0:T(2,128)S(1)}, f32[1,2,128]{2,1,0:T(2,128)S(1)}, f32[1,2,128]{2,1,0:T(2,128)S(...) while((s32[]{:T(128)}, f32[1,2,128]{2,1,0:T(2,128)S(1)}, ...), condition=%wide.region_23.36_spmd.clone, body=%wide.region_22.35_spmd.clone.sunk | while | flops 57923 | bytes 127639 | solution.py:101
  (505 shorter events, 487.1 us)
Async XLA Ops:
  1.4 35.7 %collective-permute-start.24 = (f32[1,8,512]{2,1,0:T(8,128)S(1)}, f32[1,8,512]{2,1,0:T(8,128)S(1)}, u32[]{:S(2)}, u32[]{:S(2)}) collective-permute-start(f32[1,8,512]{2,1,0:T(8,128)S(1)} %slice.468), channel_id=1, source_target_pairs={{4,0},{8,4},{12,8},{16,12},{20,16},{24,20},{28,24},{5,1},{9,5},{13... | collective-permute-start | bytes 49160 | tf_op jit(solution)/shard_map/ppermute | solution.py:26
  3.6 33.5 %collective-permute-start.25 = (f32[4,1,512]{2,1,0:T(1,128)S(1)}, f32[4,1,512]{2,1,0:T(1,128)S(1)}, u32[]{:S(2)}, u32[]{:S(2)}) collective-permute-start(f32[4,1,512]{2,1,0:T(1,128)S(1)} %slice.470), channel_id=1, source_target_pairs={{1,0},{2,1},{3,2},{5,4},{6,5},{7,6},{9,8},{10,9},{11,10},{13,12},{... | collective-permute-start | bytes 24584 | tf_op jit(solution)/shard_map/ppermute | solution.py:26
  48.3 7.1 %collective-permute-start = (f32[1,8,512]{2,1,0:T(8,128)S(1)}, f32[1,8,512]{2,1,0:T(8,128)S(1)}, u32[]{:S(2)}, u32[]{:S(2)}) collective-permute-start(f32[1,8,512]{2,1,0:T(8,128)S(1)} %get-tuple-element.988), channel_id=1, source_target_pairs={{4,0},{8,4},{12,8},{16,12},{20,16},{24,20},{28,24},{5,1},{9,5},{13... | collective-permute-start | bytes 49160 | tf_op jit(solution)/shard_map/while/body/eval_jaxpr/ppermute | solution.py:18
  71.1 7.0 %collective-permute-start.6 = (f32[6,1,512]{2,1,0:T(1,128)S(1)}, f32[6,1,512]{2,1,0:T(1,128)S(1)}, u32[]{:S(2)}, u32[]{:S(2)}) collective-permute-start(f32[6,1,512]{2,1,0:T(1,128)S(1)} %get-tuple-element.994), channel_id=1, source_target_pairs={{1,0},{2,1},{3,2},{5,4},{6,5},{7,6},{9,8},{10,9},{11,10},{13,12},{... | collective-permute-start | bytes 36872 | tf_op jit(solution)/shard_map/while/body/eval_jaxpr/ppermute | solution.py:18
  86.9 7.0 %collective-permute-start.2 = (f32[6,1,512]{2,1,0:T(1,128)S(1)}, f32[6,1,512]{2,1,0:T(1,128)S(1)}, u32[]{:S(2)}, u32[]{:S(2)}) collective-permute-start(f32[6,1,512]{2,1,0:T(1,128)S(1)} %get-tuple-element.990), channel_id=1, source_target_pairs={{1,0},{2,1},{3,2},{5,4},{6,5},{7,6},{9,8},{10,9},{11,10},{13,12},{... | collective-permute-start | bytes 36872 | tf_op jit(solution)/shard_map/while/body/eval_jaxpr/ppermute | solution.py:18
  102.6 7.0 %collective-permute-start.6 = (f32[6,1,512]{2,1,0:T(1,128)S(1)}, f32[6,1,512]{2,1,0:T(1,128)S(1)}, u32[]{:S(2)}, u32[]{:S(2)}) collective-permute-start(f32[6,1,512]{2,1,0:T(1,128)S(1)} %get-tuple-element.994), channel_id=1, source_target_pairs={{1,0},{2,1},{3,2},{5,4},{6,5},{7,6},{9,8},{10,9},{11,10},{13,12},{... | collective-permute-start | bytes 36872 | tf_op jit(solution)/shard_map/while/body/eval_jaxpr/ppermute | solution.py:18
  118.4 7.0 %collective-permute-start.2 = (f32[6,1,512]{2,1,0:T(1,128)S(1)}, f32[6,1,512]{2,1,0:T(1,128)S(1)}, u32[]{:S(2)}, u32[]{:S(2)}) collective-permute-start(f32[6,1,512]{2,1,0:T(1,128)S(1)} %get-tuple-element.990), channel_id=1, source_target_pairs={{1,0},{2,1},{3,2},{5,4},{6,5},{7,6},{9,8},{10,9},{11,10},{13,12},{... | collective-permute-start | bytes 36872 | tf_op jit(solution)/shard_map/while/body/eval_jaxpr/ppermute | solution.py:18
  134.2 7.0 %collective-permute-start.6 = (f32[6,1,512]{2,1,0:T(1,128)S(1)}, f32[6,1,512]{2,1,0:T(1,128)S(1)}, u32[]{:S(2)}, u32[]{:S(2)}) collective-permute-start(f32[6,1,512]{2,1,0:T(1,128)S(1)} %get-tuple-element.994), channel_id=1, source_target_pairs={{1,0},{2,1},{3,2},{5,4},{6,5},{7,6},{9,8},{10,9},{11,10},{13,12},{... | collective-permute-start | bytes 36872 | tf_op jit(solution)/shard_map/while/body/eval_jaxpr/ppermute | solution.py:18
  150.0 7.0 %collective-permute-start.2 = (f32[6,1,512]{2,1,0:T(1,128)S(1)}, f32[6,1,512]{2,1,0:T(1,128)S(1)}, u32[]{:S(2)}, u32[]{:S(2)}) collective-permute-start(f32[6,1,512]{2,1,0:T(1,128)S(1)} %get-tuple-element.990), channel_id=1, source_target_pairs={{1,0},{2,1},{3,2},{5,4},{6,5},{7,6},{9,8},{10,9},{11,10},{13,12},{... | collective-permute-start | bytes 36872 | tf_op jit(solution)/shard_map/while/body/eval_jaxpr/ppermute | solution.py:18
  165.7 7.0 %collective-permute-start.6 = (f32[6,1,512]{2,1,0:T(1,128)S(1)}, f32[6,1,512]{2,1,0:T(1,128)S(1)}, u32[]{:S(2)}, u32[]{:S(2)}) collective-permute-start(f32[6,1,512]{2,1,0:T(1,128)S(1)} %get-tuple-element.994), channel_id=1, source_target_pairs={{1,0},{2,1},{3,2},{5,4},{6,5},{7,6},{9,8},{10,9},{11,10},{13,12},{... | collective-permute-start | bytes 36872 | tf_op jit(solution)/shard_map/while/body/eval_jaxpr/ppermute | solution.py:18
  173.9 16.9 %collective-permute-start.26 = (f32[1,8,512]{2,1,0:T(8,128)S(1)}, f32[1,8,512]{2,1,0:T(8,128)S(1)}, u32[]{:S(2)}, u32[]{:S(2)}) collective-permute-start(f32[1,8,512]{2,1,0:T(8,128)S(1)} %get-tuple-element.774), channel_id=1, source_target_pairs={{0,4},{4,8},{8,12},{12,16},{16,20},{20,24},{24,28},{1,5},{5,9},{9,... | collective-permute-start | bytes 49160 | tf_op jit(solution)/shard_map/ppermute | solution.py:17
  195.4 9.6 %collective-permute-start.28 = (f32[6,1,512]{2,1,0:T(1,128)S(1)}, f32[6,1,512]{2,1,0:T(1,128)S(1)}, u32[]{:S(2)}, u32[]{:S(2)}) collective-permute-start(f32[6,1,512]{2,1,0:T(1,128)S(1)} %get-tuple-element.771), channel_id=1, source_target_pairs={{0,1},{1,2},{2,3},{4,5},{5,6},{6,7},{8,9},{9,10},{10,11},{12,13},{... | collective-permute-start | bytes 36872 | tf_op jit(solution)/shard_map/ppermute | solution.py:17
  239.8 7.0 %collective-permute-start.14 = (f32[4,1,256]{2,1,0:T(1,128)S(1)}, f32[4,1,256]{2,1,0:T(1,128)S(1)}, u32[]{:S(2)}, u32[]{:S(2)}) collective-permute-start(f32[4,1,256]{2,1,0:T(1,128)S(1)} %get-tuple-element.1013), channel_id=1, source_target_pairs={{1,0},{2,1},{3,2},{5,4},{6,5},{7,6},{9,8},{10,9},{11,10},{13,12},{... | collective-permute-start | bytes 12296 | tf_op jit(solution)/shard_map/while/body/eval_jaxpr/ppermute | solution.py:18
  255.2 7.0 %collective-permute-start.10 = (f32[4,1,256]{2,1,0:T(1,128)S(1)}, f32[4,1,256]{2,1,0:T(1,128)S(1)}, u32[]{:S(2)}, u32[]{:S(2)}) collective-permute-start(f32[4,1,256]{2,1,0:T(1,128)S(1)} %get-tuple-element.1009), channel_id=1, source_target_pairs={{1,0},{2,1},{3,2},{5,4},{6,5},{7,6},{9,8},{10,9},{11,10},{13,12},{... | collective-permute-start | bytes 12296 | tf_op jit(solution)/shard_map/while/body/eval_jaxpr/ppermute | solution.py:18
  270.6 7.0 %collective-permute-start.14 = (f32[4,1,256]{2,1,0:T(1,128)S(1)}, f32[4,1,256]{2,1,0:T(1,128)S(1)}, u32[]{:S(2)}, u32[]{:S(2)}) collective-permute-start(f32[4,1,256]{2,1,0:T(1,128)S(1)} %get-tuple-element.1013), channel_id=1, source_target_pairs={{1,0},{2,1},{3,2},{5,4},{6,5},{7,6},{9,8},{10,9},{11,10},{13,12},{... | collective-permute-start | bytes 12296 | tf_op jit(solution)/shard_map/while/body/eval_jaxpr/ppermute | solution.py:18
  286.1 7.0 %collective-permute-start.10 = (f32[4,1,256]{2,1,0:T(1,128)S(1)}, f32[4,1,256]{2,1,0:T(1,128)S(1)}, u32[]{:S(2)}, u32[]{:S(2)}) collective-permute-start(f32[4,1,256]{2,1,0:T(1,128)S(1)} %get-tuple-element.1009), channel_id=1, source_target_pairs={{1,0},{2,1},{3,2},{5,4},{6,5},{7,6},{9,8},{10,9},{11,10},{13,12},{... | collective-permute-start | bytes 12296 | tf_op jit(solution)/shard_map/while/body/eval_jaxpr/ppermute | solution.py:18
  301.5 7.0 %collective-permute-start.14 = (f32[4,1,256]{2,1,0:T(1,128)S(1)}, f32[4,1,256]{2,1,0:T(1,128)S(1)}, u32[]{:S(2)}, u32[]{:S(2)}) collective-permute-start(f32[4,1,256]{2,1,0:T(1,128)S(1)} %get-tuple-element.1013), channel_id=1, source_target_pairs={{1,0},{2,1},{3,2},{5,4},{6,5},{7,6},{9,8},{10,9},{11,10},{13,12},{... | collective-permute-start | bytes 12296 | tf_op jit(solution)/shard_map/while/body/eval_jaxpr/ppermute | solution.py:18
  316.9 7.0 %collective-permute-start.10 = (f32[4,1,256]{2,1,0:T(1,128)S(1)}, f32[4,1,256]{2,1,0:T(1,128)S(1)}, u32[]{:S(2)}, u32[]{:S(2)}) collective-permute-start(f32[4,1,256]{2,1,0:T(1,128)S(1)} %get-tuple-element.1009), channel_id=1, source_target_pairs={{1,0},{2,1},{3,2},{5,4},{6,5},{7,6},{9,8},{10,9},{11,10},{13,12},{... | collective-permute-start | bytes 12296 | tf_op jit(solution)/shard_map/while/body/eval_jaxpr/ppermute | solution.py:18
  332.3 7.0 %collective-permute-start.14 = (f32[4,1,256]{2,1,0:T(1,128)S(1)}, f32[4,1,256]{2,1,0:T(1,128)S(1)}, u32[]{:S(2)}, u32[]{:S(2)}) collective-permute-start(f32[4,1,256]{2,1,0:T(1,128)S(1)} %get-tuple-element.1013), channel_id=1, source_target_pairs={{1,0},{2,1},{3,2},{5,4},{6,5},{7,6},{9,8},{10,9},{11,10},{13,12},{... | collective-permute-start | bytes 12296 | tf_op jit(solution)/shard_map/while/body/eval_jaxpr/ppermute | solution.py:18
  340.3 9.2 %collective-permute-start.30 = (f32[1,4,256]{2,1,0:T(4,128)S(1)}, f32[1,4,256]{2,1,0:T(4,128)S(1)}, u32[]{:S(2)}, u32[]{:S(2)}) collective-permute-start(f32[1,4,256]{2,1,0:T(4,128)S(1)} %get-tuple-element.780), channel_id=1, source_target_pairs={{0,4},{4,8},{8,12},{12,16},{16,20},{20,24},{24,28},{1,5},{5,9},{9,... | collective-permute-start | bytes 12296 | tf_op jit(solution)/shard_map/ppermute | solution.py:17
  350.9 7.3 %collective-permute-start.32 = (f32[4,1,256]{2,1,0:T(1,128)S(1)}, f32[4,1,256]{2,1,0:T(1,128)S(1)}, u32[]{:S(2)}, u32[]{:S(2)}) collective-permute-start(f32[4,1,256]{2,1,0:T(1,128)S(1)} %get-tuple-element.777), channel_id=1, source_target_pairs={{0,1},{1,2},{2,3},{4,5},{5,6},{6,7},{8,9},{9,10},{10,11},{12,13},{... | collective-permute-start | bytes 12296 | tf_op jit(solution)/shard_map/ppermute | solution.py:17
  397.7 7.0 %collective-permute-start.18 = (f32[3,1,128]{2,1,0:T(1,128)S(1)}, f32[3,1,128]{2,1,0:T(1,128)S(1)}, u32[]{:S(2)}, u32[]{:S(2)}) collective-permute-start(f32[3,1,128]{2,1,0:T(1,128)S(1)} %get-tuple-element.1026), channel_id=1, source_target_pairs={{1,0},{2,1},{3,2},{5,4},{6,5},{7,6},{9,8},{10,9},{11,10},{13,12},{... | collective-permute-start | bytes 4616 | tf_op jit(solution)/shard_map/while/body/eval_jaxpr/ppermute | solution.py:18
  443.6 7.0 %collective-permute-start.22 = (f32[3,1,128]{2,1,0:T(1,128)S(1)}, f32[3,1,128]{2,1,0:T(1,128)S(1)}, u32[]{:S(2)}, u32[]{:S(2)}) collective-permute-start(f32[3,1,128]{2,1,0:T(1,128)S(1)} %get-tuple-element.1028), channel_id=1, source_target_pairs={{1,0},{2,1},{3,2},{5,4},{6,5},{7,6},{9,8},{10,9},{11,10},{13,12},{... | collective-permute-start | bytes 4616 | tf_op jit(solution)/shard_map/while/body/eval_jaxpr/ppermute | solution.py:18
  458.9 7.0 %collective-permute-start.18 = (f32[3,1,128]{2,1,0:T(1,128)S(1)}, f32[3,1,128]{2,1,0:T(1,128)S(1)}, u32[]{:S(2)}, u32[]{:S(2)}) collective-permute-start(f32[3,1,128]{2,1,0:T(1,128)S(1)} %get-tuple-element.1026), channel_id=1, source_target_pairs={{1,0},{2,1},{3,2},{5,4},{6,5},{7,6},{9,8},{10,9},{11,10},{13,12},{... | collective-permute-start | bytes 4616 | tf_op jit(solution)/shard_map/while/body/eval_jaxpr/ppermute | solution.py:18
  (122 other events, 771.8 us)
where the time goes:
time: 617 us; the launch traced here: 606 us
  starting transfers between devices  463 us (75%)
  local copies, waits for them, and re-layouts  62.4 us (10%)
  waiting for transfers between devices  57 us (9%)
  other arithmetic  20.3 us (3%)
    ppermute x68, starting transfers between devices, extended(): before = lax.ppermute(last, axis, up)  351 us
    ppermute x68, starting transfers between devices, extended(): after = lax.ppermute(leading, axis, down)  109 us
    ppermute x68, waiting for transfers between devices, extended(): before = lax.ppermute(last, axis, up)  47 us
    reshape x6, local copies, waits for them, and re-layouts, coarsen_face(): blocks = faces.reshape(size_x // 2, 2, size_y // 2, 2, size_z // 2, 2)  33.8 us
  transfers between devices with their start and end apart: 138, of which 68 were waited for; matrix products, arithmetic and copies ran while one was open for 8% of the time, Pallas kernels for 0%

commit v1 on v0

v1 whole, which is shorter than its diff:
```python
import functools

import jax
import jax.numpy as jnp
from jax import lax
from jax.experimental import pallas as pl
from jax.experimental.pallas import tpu as pltpu
from jax.sharding import PartitionSpec as P

SWEEPS = 4
COARSE_SWEEPS = 8
MESH = pl.DeviceIdType.MESH
F32 = jnp.float32
LANES = 128


def order_matrix(size, back):
    quarter = size // 4
    row = lax.broadcasted_iota(jnp.int32, (size, size), 1 if back else 0)
    col = lax.broadcasted_iota(jnp.int32, (size, size), 0 if back else 1)
    hit = row == 4 * (col % quarter) + col // quarter
    return jnp.where(hit, 1.0, 0.0).astype(jnp.bfloat16)


def permuted(rows, matrix):
    count = rows.shape[0]
    high = rows.astype(jnp.bfloat16)
    rest = rows - high.astype(F32)
    middle = rest.astype(jnp.bfloat16)
    low = (rest - middle.astype(F32)).astype(jnp.bfloat16)
    stacked = jnp.concatenate([high, middle, low], 0)
    out = jnp.dot(stacked, matrix, preferred_element_type=F32)
    return (out[2 * count :] + out[count : 2 * count]) + out[:count]


def kernel(
    ngx, ngy,
    rhs_ref, alpha_ref, bx_ref, by_ref, bz_ref,
    fine_ref, coarse_ref,
    l0, v0, hx, ys, hy, pairs, src_all, coef_all, l1, wx1, v1, c2, spread,
    xsend, xrecv, ysend, yrecv, gsend, grecv, csend, crecv,
):
    gx = lax.axis_index("gx")
    gy = lax.axis_index("gy")
    size_x, size_y, size_z = rhs_ref.shape
    quarter = size_z // 4
    own_p = size_y // 4
    shape0 = (size_x, 4, size_y, quarter)

    hx[...] = jnp.zeros(hx.shape, F32)
    hy[...] = jnp.zeros(hy.shape, F32)

    barrier = pltpu.get_barrier_semaphore()

    def greet_x(step, carry):
        other = lax.rem(gx + step, ngx)
        pl.semaphore_signal(barrier, inc=1, device_id=(other, gy), device_id_type=MESH)
        return carry

    def greet_y(step, carry):
        other = lax.rem(gy + step, ngy)
        pl.semaphore_signal(barrier, inc=1, device_id=(gx, other), device_id_type=MESH)
        return carry

    lax.fori_loop(1, ngx, greet_x, 0)
    lax.fori_loop(1, ngy, greet_y, 0)

    matrix = order_matrix(size_z, False)
    rows = size_x * size_y
    stacked = jnp.concatenate(
        [ref[...].reshape(rows, size_z) for ref in (rhs_ref, alpha_ref, bx_ref, by_ref, bz_ref)], 0
    )
    ordered = permuted(stacked, matrix)

    def ordered_field(number):
        whole = ordered[number * rows : (number + 1) * rows].reshape(size_x, size_y, size_z)
        return jnp.stack([whole[:, :, r * quarter : (r + 1) * quarter] for r in range(4)], 1)

    rhs, alpha, bx, by, bz = [ordered_field(number) for number in range(5)]
    RHS, INV, DIAG, WXL, WXU, WYL, WYU, WZL, WZU = range(9)
    l0[RHS] = rhs
    l0[WXL] = bx
    l0[WYL] = by

    pl.semaphore_wait(barrier, ngx - 1 + ngy - 1)

    def x_copy(slot, up, source):
        side = 0 if up else 1
        return pltpu.make_async_remote_copy(
            src_ref=source,
            dst_ref=hx.at[slot, side],
            send_sem=xsend.at[slot, side],
            recv_sem=xrecv.at[slot, side],
            device_id=(gx + 1 if up else gx - 1, gy),
            device_id_type=MESH,
        )

    def y_copy(slot, up):
        side = 0 if up else 1
        return pltpu.make_async_remote_copy(
            src_ref=ys.at[slot, side],
            dst_ref=hy.at[slot, side],
            send_sem=ysend.at[slot, side],
            recv_sem=yrecv.at[slot, side],
            device_id=(gx, gy + 1 if up else gy - 1),
            device_id_type=MESH,
        )

    has_low_x, has_high_x = gx > 0, gx < ngx - 1
    has_low_y, has_high_y = gy > 0, gy < ngy - 1

    def start_exchange(slot, field, ups=(False, True)):
        for up in ups:
            @pl.when(has_high_x if up else has_low_x)
            def _():
                x_copy(slot, up, field.at[size_x - 1 if up else 0]).start()
        for up in ups:
            @pl.when(has_high_y if up else has_low_y)
            def _():
                y_copy(slot, up).start()

    def end_exchange(slot, field, ups=(False, True)):
        for up in ups:
            @pl.when(has_low_x if up else has_high_x)
            def _():
                x_copy(slot, up, field.at[size_x - 1 if up else 0]).wait_recv()
        for up in ups:
            @pl.when(has_low_y if up else has_high_y)
            def _():
                y_copy(slot, up).wait_recv()
        for up in ups:
            @pl.when(has_high_x if up else has_low_x)
            def _():
                x_copy(slot, up, field.at[size_x - 1 if up else 0]).wait_send()
        for up in ups:
            @pl.when(has_high_y if up else has_low_y)
            def _():
                y_copy(slot, up).wait_send()

    ys[0, 1] = by[:, :, 0:1]
    start_exchange(0, l0.at[WXL], (False,))

    def pair_x(field):
        grouped = field.reshape(size_x // 2, 2, *field.shape[1:])
        return grouped[:, 0] + grouped[:, 1]

    def first_x(field):
        return field.reshape(size_x // 2, 2, *field.shape[1:])[:, 0]

    def pair_z(field):
        return jnp.stack([field[:, 0] + field[:, 1], field[:, 2] + field[:, 3]], 1)

    def first_z(field):
        return jnp.stack([field[:, 0], field[:, 2]], 1)

    def packed(field, pair_y):
        if pair_y:
            field = field + pltpu.roll(field, size_y - 1, 2)
        pairs[...] = field
        even = pairs[:, :, pl.ds(0, own_p, stride=4), :]
        odd = pairs[:, :, pl.ds(2, own_p, stride=4), :]
        return even, odd

    def put(ref, field, pair_y, scale):
        even, odd = packed(field * scale, pair_y)
        ref[:, :, 0] = even
        ref[:, :, 1] = odd

    put(coef_all.at[gy, gx, 0], pair_z(pair_x(alpha)), True, 0.125)
    put(coef_all.at[gy, gx, 1], pair_z(first_x(bx)), True, 0.0625)
    put(coef_all.at[gy, gx, 2], pair_z(pair_x(by)), False, 0.0625)
    put(coef_all.at[gy, gx, 3], first_z(pair_x(bz)), True, 0.0625)

    def row_copy(ref, ssem, rsem, other, slot):
        return pltpu.make_async_remote_copy(
            src_ref=ref.at[gy, gx], dst_ref=ref.at[gy, slot],
            send_sem=ssem.at[0, other], recv_sem=rsem.at[0, slot],
            device_id=(other, gy), device_id_type=MESH,
        )

    def column_copy(ref, ssem, rsem, other, slot):
        return pltpu.make_async_remote_copy(
            src_ref=ref.at[gy], dst_ref=ref.at[slot],
            send_sem=ssem.at[1, other], recv_sem=rsem.at[1, slot],
            device_id=(gx, other), device_id_type=MESH,
        )

    def each_other(count, me, action):
        def step(number, carry):
            action(lax.rem(me + number, count))
            return carry

        lax.fori_loop(1, count, step, 0)

    def row_start(ref, ssem, rsem):
        each_other(ngx, gx, lambda other: row_copy(ref, ssem, rsem, other, gx).start())

    def row_wait(ref, ssem, rsem):
        each_other(ngx, gx, lambda other: row_copy(ref, ssem, rsem, other, other).wait_recv())
        each_other(ngx, gx, lambda other: row_copy(ref, ssem, rsem, other, gx).wait_send())

    def column_start(ref, ssem, rsem):
        each_other(ngy, gy, lambda other: column_copy(ref, ssem, rsem, other, gy).start())

    def column_wait(ref, ssem, rsem):
        each_other(ngy, gy, lambda other: column_copy(ref, ssem, rsem, other, other).wait_recv())
        each_other(ngy, gy, lambda other: column_copy(ref, ssem, rsem, other, gy).wait_send())

    row_y = lax.broadcasted_iota(jnp.int32, shape0, 2)
    lane = lax.broadcasted_iota(jnp.int32, shape0, 3)
    residue = lax.broadcasted_iota(jnp.int32, shape0, 1)
    row_x = lax.broadcasted_iota(jnp.int32, shape0, 0)
    offset = gx * size_x + gy * size_y
    red0 = (row_x + residue + row_y + offset) % 2 == 0

    def z_lower(field):
        return jnp.concatenate([pltpu.roll(field[:, 3:], 1, 3), field[:, :3]], 1)

    def z_upper(field):
        return jnp.concatenate([field[:, 1:], pltpu.roll(field[:, :1], quarter - 1, 3)], 1)

    wzu = jnp.where((residue == 3) & (lane == quarter - 1), 0.0, z_upper(bz))
    l0[WZU] = wzu
    l0[WZL] = jnp.where((residue == 0) & (lane == 0), 0.0, bz)

    end_exchange(0, l0.at[WXL], (False,))
    row_start(coef_all, csend, crecv)
    wxu = jnp.concatenate([bx[1:], hx[0, 1][None]], 0)
    wyu = jnp.where(row_y == size_y - 1, hy[0, 1], pltpu.roll(by, size_y - 1, 2))
    l0[WXU] = wxu
    l0[WYU] = wyu
    diagonal = alpha + bx + wxu + by + wyu + bz + wzu
    l0[DIAG] = diagonal
    inverse = 1.0 / diagonal
    l0[INV] = inverse

    def beside0(slot):
        field = v0[...]
        below_x = jnp.concatenate([hx[slot, 0][None], field[:-1]], 0)
        above_x = jnp.concatenate([field[1:], hx[slot, 1][None]], 0)
        below_y = jnp.where(row_y == 0, hy[slot, 0], pltpu.roll(field, 1, 2))
        above_y = jnp.where(row_y == size_y - 1, hy[slot, 1], pltpu.roll(field, size_y - 1, 2))
        total = l0[WXL] * below_x + l0[WXU] * above_x
        total = total + (l0[WYL] * below_y + l0[WYU] * above_y)
        return total + (l0[WZL] * z_lower(field) + l0[WZU] * z_upper(field))

    def publish(slot, field):
        v0[...] = field
        ys[slot, 0] = field[:, :, size_y - 1 :]
        ys[slot, 1] = field[:, :, 0:1]
        start_exchange(slot, v0)

    publish(1, jnp.where(red0, rhs * inverse, 0.0))
    for half in range(1, 2 * SWEEPS):
        slot = half % 2
        end_exchange(slot, v0)
        updated = (l0[RHS] + beside0(slot)) * l0[INV]
        mask = red0 if half % 2 == 0 else jnp.logical_not(red0)
        publish(1 - slot, jnp.where(mask, updated, v0[...]))
        if half == 3:
            row_wait(coef_all, csend, crecv)
            column_start(coef_all, csend, crecv)
    end_exchange(0, v0)
    residual0 = l0[RHS] - (l0[DIAG] * v0[...] - beside0(0))
    put(src_all.at[gy, gx], pair_z(pair_x(residual0)), True, 0.125)
    row_start(src_all, gsend, grecv)
    column_wait(coef_all, csend, crecv)

    size_p = own_p * ngy
    shape1 = (ngx, 2, 2, 2, size_p, quarter)
    S1, INV1, DIAG1, WYL1, WZL1, UPPER1 = range(6)

    def whole_field(ref, number, block):
        parts = []
        for j in range(ngy):
            parts.append(ref[j, block] if number is None else ref[j, block, number])
        return jnp.concatenate(parts, 3)

    wx1[ngx] = jnp.zeros(shape1[1:], F32)
    v1[...] = jnp.zeros(v1.shape, F32)
    row_p = lax.broadcasted_iota(jnp.int32, shape1[2:], 2)
    lane1 = lax.broadcasted_iota(jnp.int32, shape1[2:], 3)
    half_r = lax.broadcasted_iota(jnp.int32, shape1[2:], 0)
    half_s = lax.broadcasted_iota(jnp.int32, shape1[2:], 1)

    def coefs(block, carry):
        wx1[block] = whole_field(coef_all, 1, block)
        return carry

    lax.fori_loop(0, ngx, coefs, 0)

    def more_coefs(block, carry):
        a1 = whole_field(coef_all, 0, block)
        lower_x = wx1[block]
        next_x = wx1[block + 1]
        upper_x = jnp.stack([lower_x[1], next_x[0]], 0)
        lower_y = whole_field(coef_all, 2, block)
        upper_y = jnp.stack([lower_y[:, :, 1], pltpu.roll(lower_y[:, :, 0], size_p - 1, 2)], 2)
        upper_y = jnp.where((half_s == 1) & (row_p == size_p - 1), 0.0, upper_y)
        lower_z = whole_field(coef_all, 3, block)
        upper_z = jnp.stack([lower_z[:, 1], pltpu.roll(lower_z[:, 0], quarter - 1, 3)], 1)
        upper_z = jnp.where((half_r == 1) & (lane1 == quarter - 1), 0.0, upper_z)
        diagonal1 = a1 + lower_x + upper_x + lower_y + upper_y + lower_z + upper_z
        l1[DIAG1, block] = diagonal1
        l1[INV1, block] = 1.0 / diagonal1
        l1[WYL1, block] = lower_y
        l1[UPPER1, block, :, 0] = upper_y[:, :, 1]
        l1[WZL1, block] = lower_z
        l1[UPPER1, block, :, 1] = upper_z[:, 1]
        return carry

    lax.fori_loop(0, ngx, more_coefs, 0)

    shape2 = (ngx, size_p, quarter)
    row2 = lax.broadcasted_iota(jnp.int32, shape2, 1)
    lane2 = lax.broadcasted_iota(jnp.int32, shape2, 2)
    block2 = lax.broadcasted_iota(jnp.int32, shape2, 0)
    red2 = (block2 + row2 + lane2) % 2 == 0

    def summed(ref, fixed):
        total = None
        for xl in (0, 1):
            for r in (0, 1):
                for s in (0, 1):
                    if (xl, r, s)[fixed] == 0:
                        term = ref(xl, r, s)
                        total = term if total is None else total + term
        return total

    a2_parts = None
    for j in range(ngy):
        part = None
        for xl in (0, 1):
            for r in (0, 1):
                for s in (0, 1):
                    term = coef_all[j, :, 0, xl, r, s]
                    part = term if part is None else part + term
        a2_parts = [part] if a2_parts is None else a2_parts + [part]
    a2 = jnp.concatenate(a2_parts, 1) * 0.125
    lower_x2 = summed(lambda xl, r, s: wx1[0:ngx, xl, r, s], 0) * 0.0625
    lower_y2 = summed(lambda xl, r, s: l1[WYL1, :, xl, r, s], 2) * 0.0625
    lower_z2 = summed(lambda xl, r, s: l1[WZL1, :, xl, r, s], 1) * 0.0625
    upper_x2 = jnp.concatenate([lower_x2[1:], jnp.zeros((1, size_p, quarter), F32)], 0)
    upper_y2 = jnp.where(row2 == size_p - 1, 0.0, pltpu.roll(lower_y2, size_p - 1, 1))
    upper_z2 = jnp.where(lane2 == quarter - 1, 0.0, pltpu.roll(lower_z2, quarter - 1, 2))
    diagonal2 = a2 + lower_x2 + upper_x2 + lower_y2 + upper_y2 + lower_z2 + upper_z2
    A2, WXL2, WXU2, WYL2, WYU2, WZL2, WZU2 = range(7)
    c2[A2] = 1.0 / diagonal2
    c2[WXL2] = lower_x2
    c2[WXU2] = upper_x2
    c2[WYL2] = jnp.where(row2 == 0, 0.0, lower_y2)
    c2[WYU2] = upper_y2
    c2[WZL2] = jnp.where(lane2 == 0, 0.0, lower_z2)
    c2[WZU2] = upper_z2
    for xl in (0, 1):
        for r in (0, 1):
            l1[WYL1, :, xl, r, 0] = jnp.where(row2 == 0, 0.0, l1[WYL1, :, xl, r, 0])
        for s in (0, 1):
            l1[WZL1, :, xl, 0, s] = jnp.where(lane2 == 0, 0.0, l1[WZL1, :, xl, 0, s])

    row_wait(src_all, gsend, grecv)
    column_start(src_all, gsend, grecv)
    column_wait(src_all, gsend, grecv)

    for block in range(ngx):
        l1[S1, block] = whole_field(src_all, None, block)

    def beside1(xl, r, s):
        if xl == 0:
            below_x = v1[0:ngx, 1, r, s]
            above_x = v1[1 : ngx + 1, 1, r, s]
            face_above = wx1[0:ngx, 1, r, s]
        else:
            below_x = v1[1 : ngx + 1, 0, r, s]
            above_x = v1[2 : ngx + 2, 0, r, s]
            face_above = wx1[1 : ngx + 1, 0, r, s]
        side_y = v1[1 : ngx + 1, xl, r, 1 - s]
        side_z = v1[1 : ngx + 1, xl, 1 - r, s]
        below_y = pltpu.roll(side_y, 1, 1) if s == 0 else side_y
        above_y = side_y if s == 0 else pltpu.roll(side_y, size_p - 1, 1)
        below_z = pltpu.roll(side_z, 1, 2) if r == 0 else side_z
        above_z = side_z if r == 0 else pltpu.roll(side_z, quarter - 1, 2)
        total = wx1[0:ngx, xl, r, s] * below_x + face_above * above_x
        upper_y = l1[WYL1, :, xl, r, 1] if s == 0 else l1[UPPER1, :, xl, 0, r]
        upper_z = l1[WZL1, :, xl, 1, s] if r == 0 else l1[UPPER1, :, xl, 1, s]
        total = total + (l1[WYL1, :, xl, r, s] * below_y + upper_y * above_y)
        return total + (l1[WZL1, :, xl, r, s] * below_z + upper_z * above_z)

    def half1(colour):
        for xl in (0, 1):
            for r in (0, 1):
                s = (xl + r + colour) % 2
                v1[1 : ngx + 1, xl, r, s] = (
                    l1[S1, :, xl, r, s] + beside1(xl, r, s)
                ) * l1[INV1, :, xl, r, s]

    def sweep1(number, carry):
        half1(0)
        half1(1)
        return carry

    lax.fori_loop(0, SWEEPS, sweep1, 0)

    source2 = None
    for xl in (0, 1):
        for r in (0, 1):
            for s in (0, 1):
                term = l1[S1, :, xl, r, s] - (
                    l1[DIAG1, :, xl, r, s] * v1[1 : ngx + 1, xl, r, s] - beside1(xl, r, s)
                )
                source2 = term if source2 is None else source2 + term
    source2 = source2 * 0.125

    zero_block = jnp.zeros((1, size_p, quarter), F32)

    def half2(field, mask):
        below_x = jnp.concatenate([zero_block, field[:-1]], 0)
        above_x = jnp.concatenate([field[1:], zero_block], 0)
        total = c2[WXL2] * below_x + c2[WXU2] * above_x
        total = total + (
            c2[WYL2] * pltpu.roll(field, 1, 1) + c2[WYU2] * pltpu.roll(field, size_p - 1, 1)
        )
        total = total + (
            c2[WZL2] * pltpu.roll(field, 1, 2) + c2[WZU2] * pltpu.roll(field, quarter - 1, 2)
        )
        return jnp.where(mask, (source2 + total) * c2[A2], field)

    def sweep2(number, field):
        return half2(half2(field, red2), jnp.logical_not(red2))

    coarse = lax.fori_loop(0, COARSE_SWEEPS, sweep2, jnp.zeros(shape2, F32))
    c2[A2] = coarse

    shift = lax.rem(size_p - own_p * gy, size_p)
    own_coarse = c2[A2, gx]
    coarse_ref[0] = pltpu.roll(own_coarse, shift, 0)[:own_p]
    for xl in (0, 1):
        for r in (0, 1):
            for s in (0, 1):
                tile = pltpu.roll(v1[gx + 1, xl, r, s] + own_coarse, shift, 0)[:own_p]
                spread[xl, r, pl.ds(2 * s, own_p, stride=4), :] = tile
                spread[xl, r, pl.ds(2 * s + 1, own_p, stride=4), :] = tile
    added = []
    for x in range(size_x):
        added.append(jnp.concatenate([v0[x, r] + spread[x // 2, r // 2] for r in range(4)], 1))
    natural = permuted(jnp.concatenate(added, 0), order_matrix(size_z, True))
    fine_ref[...] = natural.reshape(size_x, size_y, size_z)


def on_device(ngx, ngy, rhs, alpha, beta_x, beta_y, beta_z):
    size_x, size_y, size_z = rhs.shape
    quarter = size_z // 4
    own_p = size_y // 4
    size_p = own_p * ngy
    field0 = (size_x, 4, size_y, quarter)
    block1 = (2, 2, 2, size_p, quarter)
    piece1 = (2, 2, 2, own_p, quarter)
    dma = pltpu.SemaphoreType.DMA
    most = max(ngx, ngy)
    return pl.pallas_call(
        functools.partial(kernel, ngx, ngy),
        out_shape=(
            jax.ShapeDtypeStruct(rhs.shape, F32),
            jax.ShapeDtypeStruct((size_x // 4, own_p, quarter), F32),
        ),
        in_specs=[pl.BlockSpec(memory_space=pltpu.VMEM)] * 5,
        out_specs=(pl.BlockSpec(memory_space=pltpu.VMEM),) * 2,
        scratch_shapes=[
            pltpu.VMEM((9,) + field0, F32),
            pltpu.VMEM(field0, F32),
            pltpu.VMEM((2, 2) + field0[1:], F32),
            pltpu.VMEM((2, 2, size_x, 4, 1, quarter), F32),
            pltpu.VMEM((2, 2, size_x, 4, 1, quarter), F32),
            pltpu.VMEM((size_x // 2, 2, size_y, quarter), F32),
            pltpu.VMEM((ngy, ngx) + piece1, F32),
            pltpu.VMEM((ngy, ngx, 4) + piece1, F32),
            pltpu.VMEM((6, ngx) + block1, F32),
            pltpu.VMEM((ngx + 1,) + block1, F32),
            pltpu.VMEM((ngx + 2,) + block1, F32),
            pltpu.VMEM((7, ngx, size_p, quarter), F32),
            pltpu.VMEM((2, 2, size_y, quarter), F32),
            dma((2, 2)), dma((2, 2)), dma((2, 2)), dma((2, 2)),
            dma((2, most)), dma((2, most)), dma((2, most)), dma((2, most)),
        ],
        compiler_params=pltpu.CompilerParams(
            collective_id=0, has_side_effects=True, vmem_limit_bytes=62 * 1024 * 1024
        ),
    )(rhs, alpha, beta_x, beta_y, beta_z)


def solution(mesh):
    spec = P("gx", "gy", None)
    return jax.shard_map(
        functools.partial(on_device, mesh.shape["gx"], mesh.shape["gy"]),
        mesh=mesh,
        in_specs=(spec,) * 5,
        out_specs=(spec, spec),
        check_vma=False,
    )
```

time: 617 us -> 57.7 us (0.09); the launches traced: 606 us -> 57.5 us
  starting transfers between devices: 463 us -> 0 us
  local copies, waits for them, and re-layouts: 62.4 us -> 2.04 us
  waiting for transfers between devices: 57 us -> 0 us
  Pallas kernels: 0 us -> 54.8 us
  other arithmetic: 20.3 us -> 0 us
    ppermute x138 -> x0, starting transfers between devices: 463 us -> none  [the longest x68 351 us: extended(): before = lax.ppermute(last, axis, up)]
    ppermute x138 -> x0, waiting for transfers between devices: 57 us -> none  [the longest x68 47 us: extended(): before = lax.ppermute(last, axis, up)]
    pallas_call x0 -> x1, Pallas kernels: none -> 54.8 us  [on_device(): pl.pallas_call(functools.partial(kernel, ngx, ngy), out_shape=(jax.ShapeD...]
    reshape x10 -> x0, local copies, waits for them, and re-layouts: 45.1 us -> none  [the longest x6 33.8 us: coarsen_face(): blocks = faces.reshape(size_x // 2, 2, size_y // 2, 2, size_z // 2, 2)]
    reduce_sum x17 -> x0, other arithmetic: 12.4 us -> none  [the longest x12 7.04 us: coarsen_face(): return jnp.mean(picked, axis=others) * 0.25]
    another operation x4 -> x0, local copies, waits for them, and re-layouts: 8.56 us -> none  [coarsen_face(): picked = jnp.take(blocks, upper, axis=taken)]
  transfers between devices with their start and end apart: 138 -> 0, of which waited for: 68 -> 0; matrix products, arithmetic and copies ran while one was open for 8% -> 0% of each run, Pallas kernels for 0% -> 0%
where the time goes in v1:
time: 57.7 us; the launch traced here: 57.5 us
  Pallas kernels  54.8 us (95%)
  local copies, waits for them, and re-layouts  2.04 us (4%)
  between operations  0.65 us (1%)
    pallas_call x1, Pallas kernels, on_device(): pl.pallas_call(functools.partial(kernel, ngx, ngy), out_shape=(jax.ShapeD...  54.8 us
    unnamed x4, local copies, waits for them, and re-layouts  2.04 us

profile of v1, /device:TPU:1, one launch (start us, length us, event | category | flops | bytes accessed | tf_op | source)
XLA Modules:
  0.0 57.5 jit_solution(2160115566098783579)
XLA Ops:
  0.6 54.8 %shard_map.68 = (f32[4,8,512]{2,1,0:T(8,128)}, f32[1,2,128]{2,1,0:T(2,128)}) custom-call(f32[4,8,512]{2,1,0:T(8,128)} %rhs_ref.1, f32[4,8,512]{2,1,0:T(8,128)} %alpha_ref.1, f32[4,8,512]{2,1,0:T(8,128)} %bx_ref.1, f32[4,8,512]{2,1,0:T(8,128)} %by_ref.1, f32[4,8,512]{2,1,0:T(8,128)} %bz_ref.1), custom_call_target="tpu_custom_call" | custom-call | tf_op jit(solution)/shard_map/pallas_call | solution.py:460
  55.4 0.0 copy-start
  55.4 1.5 %copy.9 = f32[4,8,512]{2,1,0:T(8,128)} copy(f32[4,8,512]{2,1,0:T(8,128)} %get-tuple-element.4) | data formatting | bytes 131072
  56.9 0.0 copy-done
  56.9 0.6 copy.10
Async XLA Ops:
  55.4 1.5 %copy-start = (f32[1,2,128]{2,1,0:T(2,128)S(1)}, f32[1,2,128]{2,1,0:T(2,128)}, u32[]{:S(2)}) copy-start(f32[1,2,128]{2,1,0:T(2,128)} %get-tuple-element.5) | copy-start | bytes 3076

commit v2 on v1

--- a/solution.py
+++ b/solution.py
@@ -37,7 +37,7 @@
     ngx, ngy,
     rhs_ref, alpha_ref, bx_ref, by_ref, bz_ref,
     fine_ref, coarse_ref,
-    l0, v0, hx, ys, hy, pairs, src_all, coef_all, l1, wx1, v1, c2, spread,
+    l0, v0, hx, bx_in, px, qx, ys, hy, pairs, src_all, coef_all, l1, wx1, v1, c2, spread,
     xsend, xrecv, ysend, yrecv, gsend, grecv, csend, crecv,
 ):
     gx = lax.axis_index("gx")
@@ -45,9 +45,12 @@
     size_x, size_y, size_z = rhs_ref.shape
     quarter = size_z // 4
     own_p = size_y // 4
+    chips, chip, core = ngy // 2, gy // 2, lax.rem(gy, 2)
+    column = core * chips + chip
     shape0 = (size_x, 4, size_y, quarter)
 
     hx[...] = jnp.zeros(hx.shape, F32)
+    bx_in[...] = jnp.zeros(bx_in.shape, F32)
     hy[...] = jnp.zeros(hy.shape, F32)
 
     barrier = pltpu.get_barrier_semaphore()
@@ -84,11 +87,11 @@
 
     pl.semaphore_wait(barrier, ngx - 1 + ngy - 1)
 
-    def x_copy(slot, up, source):
+    def x_copy(slot, up):
         side = 0 if up else 1
         return pltpu.make_async_remote_copy(
-            src_ref=source,
-            dst_ref=hx.at[slot, side],
+            src_ref=px.at[slot, side],
+            dst_ref=qx.at[slot, side],
             send_sem=xsend.at[slot, side],
             recv_sem=xrecv.at[slot, side],
             device_id=(gx + 1 if up else gx - 1, gy),
@@ -106,39 +109,70 @@
             device_id_type=MESH,
         )
 
+    face_copy = pltpu.make_async_remote_copy(
+        src_ref=l0.at[WXL, 0],
+        dst_ref=bx_in,
+        send_sem=xsend.at[2, 0],
+        recv_sem=xrecv.at[2, 0],
+        device_id=(gx - 1, gy),
+        device_id_type=MESH,
+    )
+
     has_low_x, has_high_x = gx > 0, gx < ngx - 1
     has_low_y, has_high_y = gy > 0, gy < ngy - 1
 
-    def start_exchange(slot, field, ups=(False, True)):
-        for up in ups:
+    def strided(colour, up, r):
+        x = size_x - 1 if up else 0
+        return pl.ds((colour + x + r) % 2, size_y // 2, stride=2)
+
+    def start_exchange(slot, colour):
+        for up in (False, True):
+            side = 0 if up else 1
+            plane = size_x - 1 if up else 0
+
             @pl.when(has_high_x if up else has_low_x)
             def _():
-                x_copy(slot, up, field.at[size_x - 1 if up else 0]).start()
-        for up in ups:
+                for r in range(4):
+                    px[slot, side, r] = v0[plane, r, strided(colour, up, r), :]
+                x_copy(slot, up).start()
+        for up in (False, True):
             @pl.when(has_high_y if up else has_low_y)
             def _():
                 y_copy(slot, up).start()
 
-    def end_exchange(slot, field, ups=(False, True)):
-        for up in ups:
-            @pl.when(has_low_x if up else has_high_x)
-            def _():
-                x_copy(slot, up, field.at[size_x - 1 if up else 0]).wait_recv()
-        for up in ups:
+    def end_exchange(slot, colour):
+        for up in (False, True):
+            side = 0 if up else 1
+
             @pl.when(has_low_y if up else has_high_y)
             def _():
                 y_copy(slot, up).wait_recv()
-        for up in ups:
+
+            @pl.when(has_low_x if up else has_high_x)
+            def _():
+                x_copy(slot, up).wait_recv()
+                for r in range(4):
+                    hx[side, r, strided(colour, up, r), :] = qx[slot, side, r]
+
+    def free_slot(slot):
+        for up in (False, True):
             @pl.when(has_high_x if up else has_low_x)
             def _():
-                x_copy(slot, up, field.at[size_x - 1 if up else 0]).wait_send()
-        for up in ups:
+                x_copy(slot, up).wait_send()
+
             @pl.when(has_high_y if up else has_low_y)
             def _():
                 y_copy(slot, up).wait_send()
 
     ys[0, 1] = by[:, :, 0:1]
-    start_exchange(0, l0.at[WXL], (False,))
+
+    @pl.when(has_low_x)
+    def _():
+        face_copy.start()
+
+    @pl.when(has_low_y)
+    def _():
+        y_copy(0, False).start()
 
     def pair_x(field):
         grouped = field.reshape(size_x // 2, 2, *field.shape[1:])
@@ -166,23 +200,31 @@
         ref[:, :, 0] = even
         ref[:, :, 1] = odd
 
-    put(coef_all.at[gy, gx, 0], pair_z(pair_x(alpha)), True, 0.125)
-    put(coef_all.at[gy, gx, 1], pair_z(first_x(bx)), True, 0.0625)
-    put(coef_all.at[gy, gx, 2], pair_z(pair_x(by)), False, 0.0625)
-    put(coef_all.at[gy, gx, 3], first_z(pair_x(bz)), True, 0.0625)
+    put(coef_all.at[column, gx, 0], pair_z(pair_x(alpha)), True, 0.125)
+    put(coef_all.at[column, gx, 1], pair_z(first_x(bx)), True, 0.0625)
+    put(coef_all.at[column, gx, 2], pair_z(pair_x(by)), False, 0.0625)
+    put(coef_all.at[column, gx, 3], first_z(pair_x(bz)), True, 0.0625)
 
     def row_copy(ref, ssem, rsem, other, slot):
         return pltpu.make_async_remote_copy(
-            src_ref=ref.at[gy, gx], dst_ref=ref.at[gy, slot],
+            src_ref=ref.at[column, gx], dst_ref=ref.at[column, slot],
             send_sem=ssem.at[0, other], recv_sem=rsem.at[0, slot],
             device_id=(other, gy), device_id_type=MESH,
         )
 
     def column_copy(ref, ssem, rsem, other, slot):
         return pltpu.make_async_remote_copy(
-            src_ref=ref.at[gy], dst_ref=ref.at[slot],
+            src_ref=ref.at[column], dst_ref=ref.at[core * chips + slot],
             send_sem=ssem.at[1, other], recv_sem=rsem.at[1, slot],
-            device_id=(gx, other), device_id_type=MESH,
+            device_id=(gx, 2 * other + core), device_id_type=MESH,
+        )
+
+    def core_copy(ref, ssem, rsem, slot):
+        whole = ref.at[pl.ds(slot * chips, chips)]
+        return pltpu.make_async_remote_copy(
+            src_ref=whole, dst_ref=whole,
+            send_sem=ssem.at[2, 0], recv_sem=rsem.at[2, 0],
+            device_id=(gx, 2 * chip + 1 - core), device_id_type=MESH,
         )
 
     def each_other(count, me, action):
@@ -200,11 +242,11 @@
         each_other(ngx, gx, lambda other: row_copy(ref, ssem, rsem, other, gx).wait_send())
 
     def column_start(ref, ssem, rsem):
-        each_other(ngy, gy, lambda other: column_copy(ref, ssem, rsem, other, gy).start())
+        each_other(chips, chip, lambda other: column_copy(ref, ssem, rsem, other, chip).start())
 
     def column_wait(ref, ssem, rsem):
-        each_other(ngy, gy, lambda other: column_copy(ref, ssem, rsem, other, other).wait_recv())
-        each_other(ngy, gy, lambda other: column_copy(ref, ssem, rsem, other, gy).wait_send())
+        each_other(chips, chip, lambda other: column_copy(ref, ssem, rsem, other, other).wait_recv())
+        each_other(chips, chip, lambda other: column_copy(ref, ssem, rsem, other, chip).wait_send())
 
     row_y = lax.broadcasted_iota(jnp.int32, shape0, 2)
     lane = lax.broadcasted_iota(jnp.int32, shape0, 3)
@@ -223,9 +265,24 @@
     l0[WZU] = wzu
     l0[WZL] = jnp.where((residue == 0) & (lane == 0), 0.0, bz)
 
-    end_exchange(0, l0.at[WXL], (False,))
+    @pl.when(has_high_x)
+    def _():
+        face_copy.wait_recv()
+
+    @pl.when(has_high_y)
+    def _():
+        y_copy(0, False).wait_recv()
+
+    @pl.when(has_low_x)
+    def _():
+        face_copy.wait_send()
+
+    @pl.when(has_low_y)
+    def _():
+        y_copy(0, False).wait_send()
+
     row_start(coef_all, csend, crecv)
-    wxu = jnp.concatenate([bx[1:], hx[0, 1][None]], 0)
+    wxu = jnp.concatenate([bx[1:], bx_in[...][None]], 0)
     wyu = jnp.where(row_y == size_y - 1, hy[0, 1], pltpu.roll(by, size_y - 1, 2))
     l0[WXU] = wxu
     l0[WYU] = wyu
@@ -236,35 +293,43 @@
 
     def beside0(slot):
         field = v0[...]
-        below_x = jnp.concatenate([hx[slot, 0][None], field[:-1]], 0)
-        above_x = jnp.concatenate([field[1:], hx[slot, 1][None]], 0)
+        below_x = jnp.concatenate([hx[0][None], field[:-1]], 0)
+        above_x = jnp.concatenate([field[1:], hx[1][None]], 0)
         below_y = jnp.where(row_y == 0, hy[slot, 0], pltpu.roll(field, 1, 2))
         above_y = jnp.where(row_y == size_y - 1, hy[slot, 1], pltpu.roll(field, size_y - 1, 2))
         total = l0[WXL] * below_x + l0[WXU] * above_x
         total = total + (l0[WYL] * below_y + l0[WYU] * above_y)
         return total + (l0[WZL] * z_lower(field) + l0[WZU] * z_upper(field))
 
-    def publish(slot, field):
+    def publish(slot, colour, field):
         v0[...] = field
         ys[slot, 0] = field[:, :, size_y - 1 :]
         ys[slot, 1] = field[:, :, 0:1]
-        start_exchange(slot, v0)
-
-    publish(1, jnp.where(red0, rhs * inverse, 0.0))
+        start_exchange(slot, colour)
+
+    publish(1, 0, jnp.where(red0, rhs * inverse, 0.0))
     for half in range(1, 2 * SWEEPS):
         slot = half % 2
-        end_exchange(slot, v0)
+        end_exchange(slot, (half - 1) % 2)
         updated = (l0[RHS] + beside0(slot)) * l0[INV]
         mask = red0 if half % 2 == 0 else jnp.logical_not(red0)
-        publish(1 - slot, jnp.where(mask, updated, v0[...]))
-        if half == 3:
+        if half >= 2:
+            free_slot(1 - slot)
+        publish(1 - slot, half % 2, jnp.where(mask, updated, v0[...]))
+        if half == 2:
             row_wait(coef_all, csend, crecv)
             column_start(coef_all, csend, crecv)
-    end_exchange(0, v0)
+        if half == 5:
+            column_wait(coef_all, csend, crecv)
+            core_copy(coef_all, csend, crecv, core).start()
+    end_exchange(0, 1)
     residual0 = l0[RHS] - (l0[DIAG] * v0[...] - beside0(0))
-    put(src_all.at[gy, gx], pair_z(pair_x(residual0)), True, 0.125)
+    put(src_all.at[column, gx], pair_z(pair_x(residual0)), True, 0.125)
     row_start(src_all, gsend, grecv)
-    column_wait(coef_all, csend, crecv)
+    free_slot(1)
+    free_slot(0)
+    core_copy(coef_all, csend, crecv, 1 - core).wait_recv()
+    core_copy(coef_all, csend, crecv, core).wait_send()
 
     size_p = own_p * ngy
     shape1 = (ngx, 2, 2, 2, size_p, quarter)
@@ -273,7 +338,8 @@
     def whole_field(ref, number, block):
         parts = []
         for j in range(ngy):
-            parts.append(ref[j, block] if number is None else ref[j, block, number])
+            k = j % 2 * chips + j // 2
+            parts.append(ref[k, block] if number is None else ref[k, block, number])
         return jnp.concatenate(parts, 3)
 
     wx1[ngx] = jnp.zeros(shape1[1:], F32)
@@ -329,11 +395,12 @@
 
     a2_parts = None
     for j in range(ngy):
+        k = j % 2 * chips + j // 2
         part = None
         for xl in (0, 1):
             for r in (0, 1):
                 for s in (0, 1):
-                    term = coef_all[j, :, 0, xl, r, s]
+                    term = coef_all[k, :, 0, xl, r, s]
                     part = term if part is None else part + term
         a2_parts = [part] if a2_parts is None else a2_parts + [part]
     a2 = jnp.concatenate(a2_parts, 1) * 0.125
@@ -361,6 +428,8 @@
     row_wait(src_all, gsend, grecv)
     column_start(src_all, gsend, grecv)
     column_wait(src_all, gsend, grecv)
+    core_copy(src_all, gsend, grecv, core).start()
+    core_copy(src_all, gsend, grecv, 1 - core).wait_recv()
 
     for block in range(ngx):
         l1[S1, block] = whole_field(src_all, None, block)
@@ -428,6 +497,7 @@
     def sweep2(number, field):
         return half2(half2(field, red2), jnp.logical_not(red2))
 
+    core_copy(src_all, gsend, grecv, core).wait_send()
     coarse = lax.fori_loop(0, COARSE_SWEEPS, sweep2, jnp.zeros(shape2, F32))
     c2[A2] = coarse
 
@@ -468,7 +538,10 @@
         scratch_shapes=[
             pltpu.VMEM((9,) + field0, F32),
             pltpu.VMEM(field0, F32),
-            pltpu.VMEM((2, 2) + field0[1:], F32),
+            pltpu.VMEM((2,) + field0[1:], F32),
+            pltpu.VMEM(field0[1:], F32),
+            pltpu.VMEM((2, 2, 4, size_y // 2, quarter), F32),
+            pltpu.VMEM((2, 2, 4, size_y // 2, quarter), F32),
             pltpu.VMEM((2, 2, size_x, 4, 1, quarter), F32),
             pltpu.VMEM((2, 2, size_x, 4, 1, quarter), F32),
             pltpu.VMEM((size_x // 2, 2, size_y, quarter), F32),
@@ -479,8 +552,8 @@
             pltpu.VMEM((ngx + 2,) + block1, F32),
             pltpu.VMEM((7, ngx, size_p, quarter), F32),
             pltpu.VMEM((2, 2, size_y, quarter), F32),
-            dma((2, 2)), dma((2, 2)), dma((2, 2)), dma((2, 2)),
-            dma((2, most)), dma((2, most)), dma((2, most)), dma((2, most)),
+            dma((3, 2)), dma((3, 2)), dma((2, 2)), dma((2, 2)),
+            dma((3, most)), dma((3, most)), dma((3, most)), dma((3, most)),
         ],
         compiler_params=pltpu.CompilerParams(
             collective_id=0, has_side_effects=True, vmem_limit_bytes=62 * 1024 * 1024

time: 57.7 us -> 54.2 us (0.939)
  Pallas kernels: 54.8 us -> 51.3 us
    pallas_call x1, Pallas kernels: 54.8 us -> 51.3 us  [on_device(): pl.pallas_call(functools.partial(kernel, ngx, ngy), out_shape=(jax.ShapeD...]
where the time goes in v2:
time: 54.2 us; the launch traced here: 54 us
  Pallas kernels  51.3 us (95%)
  local copies, waits for them, and re-layouts  2.04 us (4%)
  between operations  0.65 us (1%)
    pallas_call x1, Pallas kernels, on_device(): pl.pallas_call(functools.partial(kernel, ngx, ngy), out_shape=(jax.ShapeD...  51.3 us
    unnamed x4, local copies, waits for them, and re-layouts  2.04 us

profile of v2, /device:TPU:1, one launch (start us, length us, event | category | flops | bytes accessed | tf_op | source)
XLA Modules:
  0.0 54.0 jit_solution(429361614287997572)
XLA Ops:
  0.6 51.3 %shard_map.68 = (f32[4,8,512]{2,1,0:T(8,128)}, f32[1,2,128]{2,1,0:T(2,128)}) custom-call(f32[4,8,512]{2,1,0:T(8,128)} %rhs_ref.1, f32[4,8,512]{2,1,0:T(8,128)} %alpha_ref.1, f32[4,8,512]{2,1,0:T(8,128)} %bx_ref.1, f32[4,8,512]{2,1,0:T(8,128)} %by_ref.1, f32[4,8,512]{2,1,0:T(8,128)} %bz_ref.1), custom_call_target="tpu_custom_call" | custom-call | tf_op jit(solution)/shard_map/pallas_call | solution.py:530
  51.9 0.0 copy-start
  51.9 1.5 %copy.9 = f32[4,8,512]{2,1,0:T(8,128)} copy(f32[4,8,512]{2,1,0:T(8,128)} %get-tuple-element.4) | data formatting | bytes 131072
  53.4 0.0 copy-done
  53.4 0.6 %copy.10 = f32[1,2,128]{2,1,0:T(2,128)} copy(f32[1,2,128]{2,1,0:T(2,128)S(1)} %copy-done) | data formatting | bytes 2048
Async XLA Ops:
  51.9 1.5 %copy-start = (f32[1,2,128]{2,1,0:T(2,128)S(1)}, f32[1,2,128]{2,1,0:T(2,128)}, u32[]{:S(2)}) copy-start(f32[1,2,128]{2,1,0:T(2,128)} %get-tuple-element.5) | copy-start | bytes 3076

commit v3 on v2

--- a/solution.py
+++ b/solution.py
@@ -14,22 +14,26 @@
 LANES = 128
 
 
-def order_matrix(size, back):
+def order_matrix(size):
     quarter = size // 4
-    row = lax.broadcasted_iota(jnp.int32, (size, size), 1 if back else 0)
-    col = lax.broadcasted_iota(jnp.int32, (size, size), 0 if back else 1)
-    hit = row == 4 * (col % quarter) + col // quarter
-    return jnp.where(hit, 1.0, 0.0).astype(jnp.bfloat16)
-
-
-def permuted(rows, matrix):
+    row = lax.broadcasted_iota(jnp.int32, (size, quarter), 0)
+    col = lax.broadcasted_iota(jnp.int32, (size, quarter), 1)
+    difference = row - 4 * col
+    return jnp.concatenate(
+        [jnp.where(difference == r, 1.0, 0.0).astype(jnp.bfloat16) for r in range(4)], 1
+    )
+
+
+def permuted(rows, matrix, back):
     count = rows.shape[0]
     high = rows.astype(jnp.bfloat16)
     rest = rows - high.astype(F32)
     middle = rest.astype(jnp.bfloat16)
     low = (rest - middle.astype(F32)).astype(jnp.bfloat16)
     stacked = jnp.concatenate([high, middle, low], 0)
-    out = jnp.dot(stacked, matrix, preferred_element_type=F32)
+    out = lax.dot_general(
+        stacked, matrix, (((1,), (1 if back else 0,)), ((), ())), preferred_element_type=F32
+    )
     return (out[2 * count :] + out[count : 2 * count]) + out[:count]
 
 
@@ -37,7 +41,7 @@
     ngx, ngy,
     rhs_ref, alpha_ref, bx_ref, by_ref, bz_ref,
     fine_ref, coarse_ref,
-    l0, v0, hx, bx_in, px, qx, ys, hy, pairs, src_all, coef_all, l1, wx1, v1, c2, spread,
+    l0, v0, hx, bx_in, px, qx, ys, hy, pairs, src_all, coef_all, l1, wx1, v1, c2, spread, order,
     xsend, xrecv, ysend, yrecv, gsend, grecv, csend, crecv,
 ):
     gx = lax.axis_index("gx")
@@ -68,12 +72,13 @@
     lax.fori_loop(1, ngx, greet_x, 0)
     lax.fori_loop(1, ngy, greet_y, 0)
 
-    matrix = order_matrix(size_z, False)
+    matrix = order_matrix(size_z)
+    order[...] = matrix
     rows = size_x * size_y
     stacked = jnp.concatenate(
         [ref[...].reshape(rows, size_z) for ref in (rhs_ref, alpha_ref, bx_ref, by_ref, bz_ref)], 0
     )
-    ordered = permuted(stacked, matrix)
+    ordered = permuted(stacked, matrix, False)
 
     def ordered_field(number):
         whole = ordered[number * rows : (number + 1) * rows].reshape(size_x, size_y, size_z)
@@ -253,7 +258,7 @@
     residue = lax.broadcasted_iota(jnp.int32, shape0, 1)
     row_x = lax.broadcasted_iota(jnp.int32, shape0, 0)
     offset = gx * size_x + gy * size_y
-    red0 = (row_x + residue + row_y + offset) % 2 == 0
+    red0 = ((row_x + residue + row_y + offset) & 1) == 0
 
     def z_lower(field):
         return jnp.concatenate([pltpu.roll(field[:, 3:], 1, 3), field[:, :3]], 1)
@@ -381,7 +386,7 @@
     row2 = lax.broadcasted_iota(jnp.int32, shape2, 1)
     lane2 = lax.broadcasted_iota(jnp.int32, shape2, 2)
     block2 = lax.broadcasted_iota(jnp.int32, shape2, 0)
-    red2 = (block2 + row2 + lane2) % 2 == 0
+    red2 = ((block2 + row2 + lane2) & 1) == 0
 
     def summed(ref, fixed):
         total = None
@@ -513,7 +518,7 @@
     added = []
     for x in range(size_x):
         added.append(jnp.concatenate([v0[x, r] + spread[x // 2, r // 2] for r in range(4)], 1))
-    natural = permuted(jnp.concatenate(added, 0), order_matrix(size_z, True))
+    natural = permuted(jnp.concatenate(added, 0), order[...], True)
     fine_ref[...] = natural.reshape(size_x, size_y, size_z)
 
 
@@ -552,6 +557,7 @@
             pltpu.VMEM((ngx + 2,) + block1, F32),
             pltpu.VMEM((7, ngx, size_p, quarter), F32),
             pltpu.VMEM((2, 2, size_y, quarter), F32),
+            pltpu.VMEM((size_z, size_z), jnp.bfloat16),
             dma((3, 2)), dma((3, 2)), dma((2, 2)), dma((2, 2)),
             dma((3, most)), dma((3, most)), dma((3, most)), dma((3, most)),
         ],

time: 54.2 us -> 54.2 us (level)
  no operation moved by 1% of the time
where the time goes in v3:
time: 54.2 us; the launch traced here: 54 us
  Pallas kernels  51.3 us (95%)
  local copies, waits for them, and re-layouts  2.04 us (4%)
  between operations  0.65 us (1%)
    pallas_call x1, Pallas kernels, on_device(): pl.pallas_call(functools.partial(kernel, ngx, ngy), out_shape=(jax.ShapeD...  51.3 us
    unnamed x4, local copies, waits for them, and re-layouts  2.04 us

profile of v3, /device:TPU:1, one launch (start us, length us, event | category | flops | bytes accessed | tf_op | source)
XLA Modules:
  0.0 54.0 jit_solution(9187329078458566706)
XLA Ops:
  0.6 51.3 %shard_map.68 = (f32[4,8,512]{2,1,0:T(8,128)}, f32[1,2,128]{2,1,0:T(2,128)}) custom-call(f32[4,8,512]{2,1,0:T(8,128)} %rhs_ref.1, f32[4,8,512]{2,1,0:T(8,128)} %alpha_ref.1, f32[4,8,512]{2,1,0:T(8,128)} %bx_ref.1, f32[4,8,512]{2,1,0:T(8,128)} %by_ref.1, f32[4,8,512]{2,1,0:T(8,128)} %bz_ref.1), custom_call_target="tpu_custom_call" | custom-call | tf_op jit(solution)/shard_map/pallas_call | solution.py:535
  52.0 0.0 copy-start
  52.0 1.5 %copy.9 = f32[4,8,512]{2,1,0:T(8,128)} copy(f32[4,8,512]{2,1,0:T(8,128)} %get-tuple-element.4) | data formatting | bytes 131072
  53.4 0.0 copy-done
  53.4 0.6 %copy.10 = f32[1,2,128]{2,1,0:T(2,128)} copy(f32[1,2,128]{2,1,0:T(2,128)S(1)} %copy-done) | data formatting | bytes 2048
Async XLA Ops:
  52.0 1.5 %copy-start = (f32[1,2,128]{2,1,0:T(2,128)S(1)}, f32[1,2,128]{2,1,0:T(2,128)}, u32[]{:S(2)}) copy-start(f32[1,2,128]{2,1,0:T(2,128)} %get-tuple-element.5) | copy-start | bytes 3076

commit v4 on v3

--- a/solution.py
+++ b/solution.py
@@ -51,6 +51,8 @@
     own_p = size_y // 4
     chips, chip, core = ngy // 2, gy // 2, lax.rem(gy, 2)
     column = core * chips + chip
+    pairs_x, pos_x, side_x = ngx // 2, gx // 2, lax.rem(gx, 2)
+    place = side_x * pairs_x + pos_x
     shape0 = (size_x, 4, size_y, quarter)
 
     hx[...] = jnp.zeros(hx.shape, F32)
@@ -205,10 +207,10 @@
         ref[:, :, 0] = even
         ref[:, :, 1] = odd
 
-    put(coef_all.at[column, gx, 0], pair_z(pair_x(alpha)), True, 0.125)
-    put(coef_all.at[column, gx, 1], pair_z(first_x(bx)), True, 0.0625)
-    put(coef_all.at[column, gx, 2], pair_z(pair_x(by)), False, 0.0625)
-    put(coef_all.at[column, gx, 3], first_z(pair_x(bz)), True, 0.0625)
+    put(coef_all.at[column, place, 0], pair_z(pair_x(alpha)), True, 0.125)
+    put(coef_all.at[column, place, 1], pair_z(first_x(bx)), True, 0.0625)
+    put(coef_all.at[column, place, 2], pair_z(pair_x(by)), False, 0.0625)
+    put(coef_all.at[column, place, 3], first_z(pair_x(bz)), True, 0.0625)
 
     def row_copy(ref, ssem, rsem, other, slot):
         return pltpu.make_async_remote_copy(
@@ -232,12 +234,64 @@
             device_id=(gx, 2 * chip + 1 - core), device_id_type=MESH,
         )
 
-    def each_other(count, me, action):
+    def line_copy(other, slot):
+        return pltpu.make_async_remote_copy(
+            src_ref=coef_all.at[column, place],
+            dst_ref=coef_all.at[column, side_x * pairs_x + slot],
+            send_sem=csend.at[0, other], recv_sem=crecv.at[0, slot],
+            device_id=(2 * other + side_x, gy), device_id_type=MESH,
+        )
+
+    def pair_copy(side, begin, count):
+        part = coef_all.at[column, pl.ds(side * pairs_x + begin, count)]
+        return pltpu.make_async_remote_copy(
+            src_ref=part, dst_ref=part,
+            send_sem=csend.at[3, 0], recv_sem=crecv.at[3, 0],
+            device_id=(2 * pos_x + 1 - side_x, gy), device_id_type=MESH,
+        )
+
+    def chip_copy(other, slot, begin, count):
+        return pltpu.make_async_remote_copy(
+            src_ref=coef_all.at[column, pl.ds(begin, count)],
+            dst_ref=coef_all.at[core * chips + slot, pl.ds(begin, count)],
+            send_sem=csend.at[1, other], recv_sem=crecv.at[1, slot],
+            device_id=(gx, 2 * other + core), device_id_type=MESH,
+        )
+
+    def coef_step(half):
+        if half < 2:
+            middle = (pairs_x + 1) // 2
+            low, high = ((1, middle), (middle, pairs_x))[half]
+            each_other(pairs_x, pos_x, lambda other: line_copy(other, pos_x).start(), low, high)
+        elif half < 4:
+            if half == 2:
+                each_other(pairs_x, pos_x, lambda other: line_copy(other, other).wait_recv())
+            count = pairs_x // 2
+            pair_copy(side_x, (half - 2) * count, count).start()
+        elif half < 8:
+            if half == 4:
+                pair_copy(1 - side_x, 0, pairs_x).wait_recv()
+            count = ngx // 4
+            each_other(
+                chips, chip,
+                lambda other: chip_copy(other, chip, (half - 4) * count, count).start(),
+            )
+
+    def coef_end():
+        each_other(chips, chip, lambda other: chip_copy(other, other, 0, ngx).wait_recv())
+        core_copy(coef_all, csend, crecv, core).start()
+        each_other(pairs_x, pos_x, lambda other: line_copy(other, pos_x).wait_send())
+        pair_copy(side_x, 0, pairs_x).wait_send()
+        each_other(chips, chip, lambda other: chip_copy(other, chip, 0, ngx).wait_send())
+        core_copy(coef_all, csend, crecv, 1 - core).wait_recv()
+        core_copy(coef_all, csend, crecv, core).wait_send()
+
+    def each_other(count, me, action, low=1, high=None):
         def step(number, carry):
             action(lax.rem(me + number, count))
             return carry
 
-        lax.fori_loop(1, count, step, 0)
+        lax.fori_loop(low, count if high is None else high, step, 0)
 
     def row_start(ref, ssem, rsem):
         each_other(ngx, gx, lambda other: row_copy(ref, ssem, rsem, other, gx).start())
@@ -286,7 +340,6 @@
     def _():
         y_copy(0, False).wait_send()
 
-    row_start(coef_all, csend, crecv)
     wxu = jnp.concatenate([bx[1:], bx_in[...][None]], 0)
     wyu = jnp.where(row_y == size_y - 1, hy[0, 1], pltpu.roll(by, size_y - 1, 2))
     l0[WXU] = wxu
@@ -313,6 +366,7 @@
         start_exchange(slot, colour)
 
     publish(1, 0, jnp.where(red0, rhs * inverse, 0.0))
+    coef_step(0)
     for half in range(1, 2 * SWEEPS):
         slot = half % 2
         end_exchange(slot, (half - 1) % 2)
@@ -321,30 +375,27 @@
         if half >= 2:
             free_slot(1 - slot)
         publish(1 - slot, half % 2, jnp.where(mask, updated, v0[...]))
-        if half == 2:
-            row_wait(coef_all, csend, crecv)
-            column_start(coef_all, csend, crecv)
-        if half == 5:
-            column_wait(coef_all, csend, crecv)
-            core_copy(coef_all, csend, crecv, core).start()
+        coef_step(half)
     end_exchange(0, 1)
     residual0 = l0[RHS] - (l0[DIAG] * v0[...] - beside0(0))
     put(src_all.at[column, gx], pair_z(pair_x(residual0)), True, 0.125)
     row_start(src_all, gsend, grecv)
     free_slot(1)
     free_slot(0)
-    core_copy(coef_all, csend, crecv, 1 - core).wait_recv()
-    core_copy(coef_all, csend, crecv, core).wait_send()
+    coef_end()
 
     size_p = own_p * ngy
     shape1 = (ngx, 2, 2, 2, size_p, quarter)
     S1, INV1, DIAG1, WYL1, WZL1, UPPER1 = range(6)
+
+    def slot_x(block):
+        return lax.rem(block, 2) * pairs_x + block // 2
 
     def whole_field(ref, number, block):
         parts = []
         for j in range(ngy):
             k = j % 2 * chips + j // 2
-            parts.append(ref[k, block] if number is None else ref[k, block, number])
+            parts.append(ref[k, block] if number is None else ref[k, slot_x(block), number])
         return jnp.concatenate(parts, 3)
 
     wx1[ngx] = jnp.zeros(shape1[1:], F32)
@@ -405,7 +456,9 @@
         for xl in (0, 1):
             for r in (0, 1):
                 for s in (0, 1):
-                    term = coef_all[k, :, 0, xl, r, s]
+                    term = jnp.stack(
+                        [coef_all[k, b % 2 * pairs_x + b // 2, 0, xl, r, s] for b in range(ngx)], 0
+                    )
                     part = term if part is None else part + term
         a2_parts = [part] if a2_parts is None else a2_parts + [part]
     a2 = jnp.concatenate(a2_parts, 1) * 0.125
@@ -559,7 +612,7 @@
             pltpu.VMEM((2, 2, size_y, quarter), F32),
             pltpu.VMEM((size_z, size_z), jnp.bfloat16),
             dma((3, 2)), dma((3, 2)), dma((2, 2)), dma((2, 2)),
-            dma((3, most)), dma((3, most)), dma((3, most)), dma((3, most)),
+            dma((3, most)), dma((3, most)), dma((4, most)), dma((4, most)),
         ],
         compiler_params=pltpu.CompilerParams(
             collective_id=0, has_side_effects=True, vmem_limit_bytes=62 * 1024 * 1024

time: 54.2 us -> 50.9 us (0.939)
  Pallas kernels: 51.3 us -> 48 us
    pallas_call x1, Pallas kernels: 51.3 us -> 48 us  [on_device(): pl.pallas_call(functools.partial(kernel, ngx, ngy), out_shape=(jax.ShapeD...]
where the time goes in v4:
time: 50.9 us; the launch traced here: 50.7 us
  Pallas kernels  48 us (94%)
  local copies, waits for them, and re-layouts  2.04 us (4%)
  between operations  0.65 us (1%)
    pallas_call x1, Pallas kernels, on_device(): pl.pallas_call(functools.partial(kernel, ngx, ngy), out_shape=(jax.ShapeD...  48 us
    unnamed x4, local copies, waits for them, and re-layouts  2.04 us

profile of v4, /device:TPU:1, one launch (start us, length us, event | category | flops | bytes accessed | tf_op | source)
XLA Modules:
  0.0 50.7 jit_solution(11171651989458143632)
XLA Ops:
  0.6 48.0 %shard_map.68 = (f32[4,8,512]{2,1,0:T(8,128)}, f32[1,2,128]{2,1,0:T(2,128)}) custom-call(f32[4,8,512]{2,1,0:T(8,128)} %rhs_ref.1, f32[4,8,512]{2,1,0:T(8,128)} %alpha_ref.1, f32[4,8,512]{2,1,0:T(8,128)} %bx_ref.1, f32[4,8,512]{2,1,0:T(8,128)} %by_ref.1, f32[4,8,512]{2,1,0:T(8,128)} %bz_ref.1), custom_call_target="tpu_custom_call" | custom-call | tf_op jit(solution)/shard_map/pallas_call | solution.py:588
  48.6 0.0 copy-start
  48.6 1.5 %copy.9 = f32[4,8,512]{2,1,0:T(8,128)} copy(f32[4,8,512]{2,1,0:T(8,128)} %get-tuple-element.4) | data formatting | bytes 131072
  50.1 0.0 copy-done
  50.1 0.6 %copy.10 = f32[1,2,128]{2,1,0:T(2,128)} copy(f32[1,2,128]{2,1,0:T(2,128)S(1)} %copy-done) | data formatting | bytes 2048
Async XLA Ops:
  48.6 1.5 %copy-start = (f32[1,2,128]{2,1,0:T(2,128)S(1)}, f32[1,2,128]{2,1,0:T(2,128)}, u32[]{:S(2)}) copy-start(f32[1,2,128]{2,1,0:T(2,128)} %get-tuple-element.5) | copy-start | bytes 3076

commit v5 on v4

--- a/solution.py
+++ b/solution.py
@@ -383,6 +383,8 @@
     free_slot(1)
     free_slot(0)
     coef_end()
+    row_wait(src_all, gsend, grecv)
+    column_start(src_all, gsend, grecv)
 
     size_p = own_p * ngy
     shape1 = (ngx, 2, 2, 2, size_p, quarter)
@@ -431,7 +433,12 @@
         l1[UPPER1, block, :, 1] = upper_z[:, 1]
         return carry
 
-    lax.fori_loop(0, ngx, more_coefs, 0)
+    def two_blocks(number, carry):
+        return more_coefs(2 * number + 1, more_coefs(2 * number, carry))
+
+    lax.fori_loop(0, ngx // 2, two_blocks, 0)
+    column_wait(src_all, gsend, grecv)
+    core_copy(src_all, gsend, grecv, core).start()
 
     shape2 = (ngx, size_p, quarter)
     row2 = lax.broadcasted_iota(jnp.int32, shape2, 1)
@@ -483,10 +490,6 @@
         for s in (0, 1):
             l1[WZL1, :, xl, 0, s] = jnp.where(lane2 == 0, 0.0, l1[WZL1, :, xl, 0, s])
 
-    row_wait(src_all, gsend, grecv)
-    column_start(src_all, gsend, grecv)
-    column_wait(src_all, gsend, grecv)
-    core_copy(src_all, gsend, grecv, core).start()
     core_copy(src_all, gsend, grecv, 1 - core).wait_recv()
 
     for block in range(ngx):

time: 50.9 us -> 50.9 us (level)
  no operation moved by 1% of the time
where the time goes in v5:
time: 50.9 us; the launch traced here: 50.6 us
  Pallas kernels  48 us (94%)
  local copies, waits for them, and re-layouts  2.04 us (4%)
  between operations  0.65 us (1%)
    pallas_call x1, Pallas kernels, on_device(): pl.pallas_call(functools.partial(kernel, ngx, ngy), out_shape=(jax.ShapeD...  48 us
    unnamed x4, local copies, waits for them, and re-layouts  2.04 us

profile of v5, /device:TPU:1, one launch (start us, length us, event | category | flops | bytes accessed | tf_op | source)
XLA Modules:
  0.0 50.6 jit_solution(12639892763053094889)
XLA Ops:
  0.6 48.0 %shard_map.68 = (f32[4,8,512]{2,1,0:T(8,128)}, f32[1,2,128]{2,1,0:T(2,128)}) custom-call(f32[4,8,512]{2,1,0:T(8,128)} %rhs_ref.1, f32[4,8,512]{2,1,0:T(8,128)} %alpha_ref.1, f32[4,8,512]{2,1,0:T(8,128)} %bx_ref.1, f32[4,8,512]{2,1,0:T(8,128)} %by_ref.1, f32[4,8,512]{2,1,0:T(8,128)} %bz_ref.1), custom_call_target="tpu_custom_call" | custom-call | tf_op jit(solution)/shard_map/pallas_call | solution.py:591
  48.6 0.0 copy-start
  48.6 1.5 %copy.9 = f32[4,8,512]{2,1,0:T(8,128)} copy(f32[4,8,512]{2,1,0:T(8,128)} %get-tuple-element.4) | data formatting | bytes 131072
  50.1 0.0 copy-done
  50.1 0.6 %copy.10 = f32[1,2,128]{2,1,0:T(2,128)} copy(f32[1,2,128]{2,1,0:T(2,128)S(1)} %copy-done) | data formatting | bytes 2048
Async XLA Ops:
  48.6 1.5 %copy-start = (f32[1,2,128]{2,1,0:T(2,128)S(1)}, f32[1,2,128]{2,1,0:T(2,128)}, u32[]{:S(2)}) copy-start(f32[1,2,128]{2,1,0:T(2,128)} %get-tuple-element.5) | copy-start | bytes 3076
